TPU v7x, 512 devices: a whole 4x8x8 slice. The times are simulated.
512 devices in a mesh: row: 32 (over z, x), col: 16 (over y, core).
Axes of the slice: x: 4, y: 8, z: 8, core: 2. Of those that a mesh axis runs over, the one named last changes fastest.
Arguments:
- images: bfloat16 [4096, 1152], P('row'), may hold values from -4 to 4
- captions: bfloat16 [32768, 1152], P('col'), may hold values from -4 to 4
Outputs:
- image_dual: float32 [4096], P('row')
- caption_dual: float32 [32768], P('col')
- mapped: float32 [4096, 1152], P('row', 'col')
All inputs are finite; a program needn't handle non-finite values.
Results may differ from a plain program's by a relative error of at most 0.0023.
Values sent between devices are 32-bit elements; how exact they have to be, the bound alone decides.
A program may use at most 64 MiB of HBM per device.

v0:
```python
import math

import jax
import jax.numpy as jnp
from jax import lax
from jax.sharding import PartitionSpec as P

ITERS = 2


entropic = 0.05


def joined(part, axis, combine):
    gathered = jax.tree.map(lambda a: lax.all_gather(a, axis), part)

    def take(source):
        return jax.tree.map(lambda a: lax.dynamic_index_in_dim(a, source, 0, False), gathered)

    return lax.fori_loop(
        1, lax.axis_size(axis), lambda source, state: combine(state, take(source)), take(0)
    )


def similarity(images, captions):
    return lax.dot_general(
        images, captions, (((1,), (1,)), ((), ())), preferred_element_type=jnp.float32
    )


def combine_three(first, second):
    top = jnp.maximum(first[0], second[0])
    left = jnp.exp(first[0] - top)
    right = jnp.exp(second[0] - top)
    return (
        top,
        first[1] * left + second[1] * right,
        first[2] * left[:, None] + second[2] * right[:, None],
    )


def image_lse(logits):
    local_max = jnp.max(logits, axis=1)
    top = lax.pmax(local_max, "col")
    total = lax.psum(jnp.sum(jnp.exp(logits - top[:, None]), axis=1), "col")
    return top + jnp.log(total)


def caption_lse(logits):
    local_max = jnp.max(logits, axis=0)
    top = lax.pmax(local_max, "row")
    total = lax.psum(jnp.sum(jnp.exp(logits - top[None, :]), axis=0), "row")
    return top + jnp.log(total)


def per_device(images, captions):
    rows_here = images.shape[0]
    cols_here = captions.shape[0]
    width = images.shape[1]
    col_count = lax.axis_size("col")
    log_a = jnp.float32(-math.log(rows_here * lax.axis_size("row")))
    log_b = jnp.float32(-math.log(cols_here * col_count))
    caption_dual = jnp.zeros((cols_here,), jnp.float32)
    image_dual = jnp.zeros((rows_here,), jnp.float32)
    for step in range(ITERS):
        logits = (caption_dual[None, :] + similarity(images, captions)) / entropic
        image_dual = entropic * log_a - entropic * image_lse(logits)
        logits = (image_dual[:, None] + similarity(images, captions)) / entropic
        caption_dual = entropic * log_b - entropic * caption_lse(logits)
    logits = (caption_dual[None, :] + similarity(images, captions)) / entropic
    local_max = jnp.max(logits, axis=1)
    share = width // col_count
    weights = jnp.exp(logits - local_max[:, None])
    mass = jnp.sum(weights, axis=1)
    numer = jnp.dot(weights.astype(jnp.bfloat16), captions, preferred_element_type=jnp.float32)
    top, mass, numer = joined((local_max, mass, numer), "col", combine_three)
    mapped = numer / mass[:, None]
    mapped = lax.dynamic_slice_in_dim(mapped, lax.axis_index("col") * share, share, 1)
    return (image_dual, caption_dual, mapped)


def solution(mesh):
    return jax.shard_map(
        per_device,
        mesh=mesh,
        in_specs=(P("row", None), P("col", None)),
        out_specs=(P("row"), P("col"), P("row", "col")),
        check_vma=False,
    )
```

profile of v0, /device:TPU:1, one launch (start us, length us, event | category | flops | bytes accessed | tf_op | source)
XLA Modules:
  0.0 497.0 jit_solution(4928959867055213251)
XLA Ops:
  7.2 0.0 copy-start
  7.2 0.0 all-gather.7.cloned.1.call-start
  7.2 0.9 copy-done
  8.1 4.0 multiply_reduce_fusion
  12.2 29.8 %pmax.28 = f32[128]{0:T(128)S(1)} all-reduce(f32[128]{0:T(128)S(1)} %get-tuple-element.200), channel_id=1, replica_groups=mesh['row'=32,'col'=16] {'col'}, use_global_device_ids=true, to_apply=%region_1.0 | all-reduce | flops 128 | bytes 1024 | tf_op jit(solution)/shard_map/pmax | solution.py:44
  41.9 0.3 exponential_reduce_fusion.3
  42.3 23.5 %psum.28 = f32[128]{0:T(128)S(1)} all-reduce(f32[128]{0:T(128)S(1)} %exponential_reduce_fusion.3), channel_id=1, replica_groups=mesh['row'=32,'col'=16] {'col'}, use_global_device_ids=true, to_apply=%region_3.0 | all-reduce | flops 128 | bytes 1024 | tf_op jit(solution)/shard_map/psum | solution.py:45
  65.8 0.2 fusion.6
  66.0 65.2 %pmax.29 = f32[2048]{0:T(1024)S(1)} all-reduce(f32[2048]{0:T(1024)S(1)} %fusion.6), channel_id=1, replica_groups=mesh['row'=32,'col'=16] {'row'}, use_global_device_ids=true, to_apply=%region_5.0 | all-reduce | flops 2048 | bytes 16384 | tf_op jit(solution)/shard_map/pmax | solution.py:51
  131.2 0.3 exponential_reduce_fusion.2
  131.5 56.8 %psum.29 = f32[2048]{0:T(1024)S(1)} all-reduce(f32[2048]{0:T(1024)S(1)} %exponential_reduce_fusion.2), channel_id=1, replica_groups=mesh['row'=32,'col'=16] {'row'}, use_global_device_ids=true, to_apply=%region_7.0 | all-reduce | flops 2048 | bytes 16384 | tf_op jit(solution)/shard_map/psum | solution.py:52
  188.4 0.2 fusion.7
  188.6 51.5 %pmax.30 = f32[128]{0:T(128)S(1)} all-reduce(f32[128]{0:T(128)S(1)} %fusion.7), channel_id=1, replica_groups=mesh['row'=32,'col'=16] {'col'}, use_global_device_ids=true, to_apply=%region_9.0 | all-reduce | flops 128 | bytes 1024 | tf_op jit(solution)/shard_map/pmax | solution.py:44
  240.1 0.3 exponential_reduce_fusion.1
  240.5 23.5 %psum.30 = f32[128]{0:T(128)S(1)} all-reduce(f32[128]{0:T(128)S(1)} %exponential_reduce_fusion.1), channel_id=1, replica_groups=mesh['row'=32,'col'=16] {'col'}, use_global_device_ids=true, to_apply=%region_11.0 | all-reduce | flops 128 | bytes 1024 | tf_op jit(solution)/shard_map/psum | solution.py:45
  264.0 0.2 fusion.8
  264.2 59.1 %pmax.31 = f32[2048]{0:T(1024)S(1)} all-reduce(f32[2048]{0:T(1024)S(1)} %fusion.8), channel_id=1, replica_groups=mesh['row'=32,'col'=16] {'row'}, use_global_device_ids=true, to_apply=%region_13.0 | all-reduce | flops 2048 | bytes 16384 | tf_op jit(solution)/shard_map/pmax | solution.py:51
  323.4 0.3 exponential_reduce_fusion
  323.7 57.1 %psum.31 = f32[2048]{0:T(1024)S(1)} all-reduce(f32[2048]{0:T(1024)S(1)} %exponential_reduce_fusion), channel_id=1, replica_groups=mesh['row'=32,'col'=16] {'row'}, use_global_device_ids=true, to_apply=%region_15.0 | all-reduce | flops 2048 | bytes 16384 | tf_op jit(solution)/shard_map/psum | solution.py:52
  380.7 0.0 copy-start.1
  380.8 0.2 fusion.9
  380.9 4.1 fusion.12
  385.0 0.0 copy-done.2
  385.0 0.0 all-gather.7.cloned.1.call-update
  385.1 41.7 %all-gather.3 = f32[16,1,128]{2,1,0:T(1,128)S(1)} all-gather(f32[1,1,128]{2,1,0:T(1,128)S(1)} %bitcast.37), channel_id=2, replica_groups=mesh['row'=32,'col'=16] {'col'}, dimensions={0}, use_global_device_ids=true | all-gather | bytes 8704 | tf_op jit(solution)/shard_map/all_gather | solution.py:15
  426.8 0.3 fusion.11
  427.1 16.0 %all-gather.4 = f32[16,1,128]{2,1,0:T(1,128)S(1)} all-gather(f32[1,1,128]{2,1,0:T(1,128)S(1)} %bitcast.38), channel_id=3, replica_groups=mesh['row'=32,'col'=16] {'col'}, dimensions={0}, use_global_device_ids=true | all-gather | bytes 8704 | tf_op jit(solution)/shard_map/all_gather | solution.py:15
  443.1 25.2 %all-gather.7.cloned.1.call-done = f32[2048,1152]{1,0:T(8,128)} async-done(((f32[128,1152]{1,0:T(8,128)}), f32[2048,1152]{1,0:T(8,128)}) %all-gather.7.cloned.1.call-update) | async-done | bytes 9437200 | tf_op jit(solution)/shard_map/all_gather | solution.py:15
  468.3 1.1 slice.10
  469.4 0.0 copy-done.1
  469.4 19.9 %while.19 = (s32[]{:T(128)}, f32[128]{0:T(128)S(1)}, f32[128]{0:T(128)S(1)}, f32[128,1152]{1,0:T(8,128)S(1)}, f32[16,128]{1,0:T(8,128)S(1)}, /*index=5*/f32[16,1...) while((s32[]{:T(128)}, f32[128]{0:T(128)S(1)}, f32[128]{0:T(128)S(1)}, ...), condition=%wide.region_19.20_spmd, body=%wide.region_18.19_spmd.sunk | while | flops 443141 | bytes 1774743 | solution.py:20
  469.5 1.3 fusion.25
  470.8 1.3 fusion.25
  472.1 1.3 fusion.25
  473.4 1.3 fusion.25
  474.8 1.3 fusion.25
  476.1 1.3 fusion.25
  477.4 1.3 fusion.25
  478.7 1.3 fusion.25
  480.1 1.3 fusion.25
  481.4 1.3 fusion.25
  482.7 1.3 fusion.25
  484.0 1.3 fusion.25
  485.4 1.3 fusion.25
  486.7 1.3 fusion.25
  488.0 1.3 fusion.25
  489.3 0.2 copy.6
  489.5 0.6 dynamic-slice_divide_fusion
  (22 shorter events, 0.5 us)
Async XLA Ops:
  7.2 1.0 copy-start
  7.2 461.1 %all-gather.7.cloned.1.call-start = ((), (), s32[]{:S(2)}) async-start(), calls=%async_computation | async-start | bytes 10027008 | tf_op jit(solution)/shard_map/all_gather | solution.py:15
  264.0 121.0 %copy-start.2 = (f32[128]{0:T(128)}, f32[128]{0:T(128)S(1)}, u32[]{:S(2)}) copy-start(f32[128]{0:T(128)S(1)} %multiply_subtract_fusion.2) | copy-start | bytes 1540
  380.7 88.7 %copy-start.1 = (f32[2048]{0:T(1024)}, f32[2048]{0:T(1024)S(1)}, u32[]{:S(2)}) copy-start(f32[2048]{0:T(1024)S(1)} %multiply_subtract_fusion) | copy-start | bytes 24580
Sparse Core Ops, SparseCore 0:
  385.2 83.0 all-gather.6
where the time goes:
time: 498 us; the launch traced here: 497 us
  blocking collectives  424 us (85%)
  waiting for transfers between devices  25.2 us (5%)
  other arithmetic  22.4 us (4%)
  between operations  14.2 us (3%)
  matrix products  8.12 us (2%)
    pmax x2, blocking collectives, caption_lse(): top = lax.pmax(local_max, 'row')  124 us
    psum x2, blocking collectives, caption_lse(): total = lax.psum(jnp.sum(jnp.exp(logits - top[None, :]), axis=0), 'row')  114 us
    pmax x2, blocking collectives, image_lse(): top = lax.pmax(local_max, 'col')  81.3 us
    all_gather x2, blocking collectives, joined(): gathered = jax.tree.map(lambda a: lax.all_gather(a, axis), part)  57.7 us
    psum x2, blocking collectives, image_lse(): total = lax.psum(jnp.sum(jnp.exp(logits - top[:, None]), axis=1), 'col')  47.1 us
    all_gather x1, waiting for transfers between devices, joined(): gathered = jax.tree.map(lambda a: lax.all_gather(a, axis), part)  25.2 us
    add x15, other arithmetic, combine_three(): first[2] * left[:, None] + second[2] * right[:, None]  19 us
  transfers between devices with their start and end apart: 1, of which 1 were waited for; matrix products, arithmetic and copies ran while one was open for 0% of the time, Pallas kernels for 0%

commit v1 on v0

v1 whole, which is shorter than its diff:
```python
import functools
import math

import jax
import jax.numpy as jnp
from jax import lax
from jax.experimental import pallas as pl
from jax.experimental.pallas import tpu as pltpu
from jax.sharding import PartitionSpec as P

MESH = pl.DeviceIdType.MESH
ENTROPIC = 0.05
LOG2E = math.log2(math.e)
ITERS = 2
LANES = 128
GROUP = 16
X_CHIPS = 4


def ring(offset, size):
    return min(offset, size - offset)


def tree(op, values):
    values = list(values)
    while len(values) > 1:
        rest = [op(a, b) for a, b in zip(values[::2], values[1::2])]
        values = rest + ([values[-1]] if len(values) % 2 else [])
    return values[0]


def lse_of(parts):
    top = tree(jnp.maximum, parts)
    return top + jnp.log2(tree(jnp.add, [jnp.exp2(p - top) for p in parts]))


def kernel(
    rows_n, cols_n, images_hbm, captions_hbm, image_out, caption_out, mapped_out,
    images, captions, score, weights, stat_max, stat_sum, block_max, block_sum, dual,
    image_src, image_recv, caption_src, caption_recv, numer, pair_recv, y_src, y_recv,
    load_sem, image_ssem, image_rsem, caption_ssem, caption_rsem,
    pair_ssem, pair_rsem, y_ssem, y_rsem,
):
    here, width = images.shape
    blocks = score.shape[1] // LANES
    loads = captions.shape[0] // 256
    x_n = X_CHIPS
    z_n = rows_n // x_n
    y_n = cols_n // 2
    share = width // cols_n
    r, c = lax.axis_index("row"), lax.axis_index("col")
    z, x, y, core = r // x_n, lax.rem(r, x_n), c // 2, lax.rem(c, 2)

    def row_peer(dz, dx):
        return (lax.rem(z + dz, z_n) * x_n + lax.rem(x + dx, x_n), c)

    def col_peer(dy, dc):
        return (r, lax.rem(y + dy, y_n) * 2 + lax.rem(core + dc, 2))

    row_peers = sorted(
        [(dz, dx) for dz in range(z_n) for dx in range(x_n) if dz or dx],
        key=lambda p: -ring(p[0], z_n) - ring(p[1], x_n),
    )
    col_peers = sorted(
        [(dy, dc) for dy in range(y_n) for dc in range(2) if dy or dc],
        key=lambda p: -ring(p[0], y_n) - 0.5 * p[1],
    )
    y_peers = sorted(range(1, y_n), key=lambda p: -ring(p, y_n))

    image_load = pltpu.make_async_copy(images_hbm, images, load_sem.at[loads])
    image_load.start()
    caption_loads = []
    for b in range(loads):
        part = pl.ds(b * 256, 256)
        caption_loads.append(
            pltpu.make_async_copy(captions_hbm.at[part], captions.at[part], load_sem.at[b])
        )
        caption_loads[-1].start()

    barrier = pltpu.get_barrier_semaphore()
    for p in row_peers:
        pl.semaphore_signal(barrier, inc=1, device_id=row_peer(*p), device_id_type=MESH)
    for p in col_peers:
        pl.semaphore_signal(barrier, inc=1, device_id=col_peer(*p), device_id_type=MESH)

    image_load.wait()
    for b in range(loads):
        caption_loads[b].wait()
        part = pl.ds(b * 256, 256)
        score[:, part] = lax.dot_general(
            images[...], captions[part, :], (((1,), (1,)), ((), ())),
            preferred_element_type=jnp.float32,
        ) * jnp.float32(LOG2E / ENTROPIC)

    log_a = jnp.float32(-math.log2(here * rows_n))
    log_b = jnp.float32(-math.log2(score.shape[1] * cols_n))

    def logit_rows(g, with_dual):
        rows = pl.ds(g * GROUP, GROUP)
        out = []
        for b in range(blocks):
            v = score[rows, pl.ds(b * LANES, LANES)]
            out.append(v + dual[pl.ds(b, 1), :] if with_dual else v)
        return rows, out

    def send_image(step):
        for k, p in enumerate(col_peers):
            pltpu.make_async_remote_copy(
                src_ref=image_src.at[step], dst_ref=image_recv.at[step, k],
                send_sem=image_ssem.at[step], recv_sem=image_rsem.at[step],
                device_id=col_peer(*p), device_id_type=MESH,
            ).start()

    def get_image(step):
        whole = image_recv.at[step]
        pltpu.make_async_copy(whole, whole, image_rsem.at[step]).wait()
        return lse_of(
            [image_src[step]] + [image_recv[step, k] for k in range(len(col_peers))]
        )

    for step in range(ITERS):
        for g in range(here // GROUP):
            rows, logits = logit_rows(g, step > 0)
            top = tree(jnp.maximum, logits)
            stat_max[rows, :] = top
            stat_sum[rows, :] = tree(jnp.add, [jnp.exp2(v - top) for v in logits])
        lane_max = stat_max[...].T
        top = jnp.max(lane_max, axis=0, keepdims=True)
        total = jnp.sum(stat_sum[...].T * jnp.exp2(lane_max - top), axis=0, keepdims=True)
        image_src[step] = top + jnp.log2(total)
        if step == 0:
            pl.semaphore_wait(barrier, len(row_peers) + len(col_peers))
        send_image(step)
        image_dual = log_a - get_image(step)
        if step == ITERS - 1:
            image_out[...] = image_dual * jnp.float32(ENTROPIC / LOG2E)
        column = jnp.broadcast_to(image_dual, (LANES, here)).T
        for b in range(blocks):
            logits = score[:, pl.ds(b * LANES, LANES)] + column
            top = jnp.max(logits, axis=0, keepdims=True)
            block_max[pl.ds(b, 1), :] = top
            block_sum[pl.ds(b, 1), :] = jnp.sum(jnp.exp2(logits - top), axis=0, keepdims=True)
        caption_src[step] = block_max[...] + jnp.log2(block_sum[...])
        for k, p in enumerate(row_peers):
            pltpu.make_async_remote_copy(
                src_ref=caption_src.at[step], dst_ref=caption_recv.at[step, k],
                send_sem=caption_ssem.at[step], recv_sem=caption_rsem.at[step],
                device_id=row_peer(*p), device_id_type=MESH,
            ).start()
        whole = caption_recv.at[step]
        pltpu.make_async_copy(whole, whole, caption_rsem.at[step]).wait()
        dual[...] = log_b - lse_of(
            [caption_src[step]] + [caption_recv[step, k] for k in range(len(row_peers))]
        )

    caption_out[...] = dual[...] * jnp.float32(ENTROPIC / LOG2E)
    for g in range(here // GROUP):
        rows, logits = logit_rows(g, True)
        top = jnp.max(tree(jnp.maximum, logits), axis=1, keepdims=True)
        stat_max[rows, :] = jnp.broadcast_to(top, (GROUP, LANES))
        terms = [jnp.exp2(v - top) for v in logits]
        stat_sum[rows, :] = tree(jnp.add, terms)
        for b, w in enumerate(terms):
            weights[rows, pl.ds(b * LANES, LANES)] = w.astype(jnp.bfloat16)
    own_top = stat_max[...].T[0:1, :]
    mass = jnp.sum(stat_sum[...].T, axis=0, keepdims=True)
    image_src[ITERS] = own_top + jnp.log2(mass)
    send_image(ITERS)

    for b in range(width // LANES):
        part = pl.ds(b * LANES, LANES)
        numer[part, :] = jnp.dot(
            weights[...], captions[:, part], preferred_element_type=jnp.float32
        ).T
    factor = jnp.exp2(own_top - get_image(ITERS))

    def chunk(dy, of_core):
        start = (lax.rem(y + dy, y_n) * 2 + of_core) * share
        return pl.ds(pl.multiple_of(start, 8), share)

    pair_order = y_peers + [0]
    for dy in pair_order:
        part = chunk(dy, 1 - core)
        numer[part, :] = numer[part, :] * factor
        pltpu.make_async_remote_copy(
            src_ref=numer.at[part], dst_ref=pair_recv.at[dy],
            send_sem=pair_ssem, recv_sem=pair_rsem.at[dy],
            device_id=col_peer(0, 1), device_id_type=MESH,
        ).start()
    copies = []
    for dy in pair_order:
        pltpu.make_async_copy(pair_recv.at[dy], pair_recv.at[dy], pair_rsem.at[dy]).wait()
        y_src[dy] = numer[chunk(dy, core), :] * factor + pair_recv[dy]
        if dy:
            copies.append(
                pltpu.make_async_remote_copy(
                    src_ref=y_src.at[dy], dst_ref=y_recv.at[dy - 1],
                    send_sem=y_ssem, recv_sem=y_rsem.at[dy - 1],
                    device_id=col_peer(dy, 0), device_id_type=MESH,
                )
            )
            copies[-1].start()
    total = y_src[0]
    for dy in reversed(y_peers):
        pltpu.make_async_copy(y_recv.at[dy - 1], y_recv.at[dy - 1], y_rsem.at[dy - 1]).wait()
        total = total + y_recv[dy - 1]
    mapped_out[...] = total

    for step in range(ITERS + 1):
        whole = image_recv.at[step]
        pltpu.make_async_copy(whole, whole, image_ssem.at[step]).wait()
    for step in range(ITERS):
        whole = caption_recv.at[step]
        pltpu.make_async_copy(whole, whole, caption_ssem.at[step]).wait()
    pltpu.make_async_copy(pair_recv, pair_recv, pair_ssem).wait()
    pltpu.make_async_copy(y_recv, y_recv, y_ssem).wait()


def solution(mesh):
    rows_n, cols_n = mesh.shape["row"], mesh.shape["col"]
    y_n = cols_n // 2

    def per_device(images, captions):
        here, width = images.shape
        cols = captions.shape[0]
        share = width // cols_n
        blocks = cols // LANES
        f32 = jnp.float32
        vmem = pl.BlockSpec(memory_space=pltpu.VMEM)
        dma = pltpu.SemaphoreType.DMA
        image_dual, caption_dual, mapped = pl.pallas_call(
            functools.partial(kernel, rows_n, cols_n),
            out_shape=(
                jax.ShapeDtypeStruct((1, here), f32),
                jax.ShapeDtypeStruct((blocks, LANES), f32),
                jax.ShapeDtypeStruct((share, here), f32),
            ),
            in_specs=[pl.BlockSpec(memory_space=pl.ANY)] * 2,
            out_specs=(vmem, vmem, vmem),
            scratch_shapes=[
                pltpu.VMEM((here, width), jnp.bfloat16),
                pltpu.VMEM((cols, width), jnp.bfloat16),
                pltpu.VMEM((here, cols), f32),
                pltpu.VMEM((here, cols), jnp.bfloat16),
                pltpu.VMEM((here, LANES), f32),
                pltpu.VMEM((here, LANES), f32),
                pltpu.VMEM((blocks, LANES), f32),
                pltpu.VMEM((blocks, LANES), f32),
                pltpu.VMEM((blocks, LANES), f32),
                pltpu.VMEM((ITERS + 1, 1, here), f32),
                pltpu.VMEM((ITERS + 1, cols_n - 1, 1, here), f32),
                pltpu.VMEM((ITERS, blocks, LANES), f32),
                pltpu.VMEM((ITERS, rows_n - 1, blocks, LANES), f32),
                pltpu.VMEM((width, here), f32),
                pltpu.VMEM((y_n, share, here), f32),
                pltpu.VMEM((y_n, share, here), f32),
                pltpu.VMEM((y_n - 1, share, here), f32),
                dma((cols // 256 + 1,)),
                dma((ITERS + 1,)),
                dma((ITERS + 1,)),
                dma((ITERS,)),
                dma((ITERS,)),
                dma,
                dma((y_n,)),
                dma,
                dma((y_n - 1,)),
            ],
            compiler_params=pltpu.CompilerParams(
                collective_id=0, has_side_effects=True, vmem_limit_bytes=60 * 2**20
            ),
            name="sinkhorn",
        )(images, captions)
        return image_dual.reshape(here), caption_dual.reshape(cols), mapped.T

    return jax.shard_map(
        per_device,
        mesh=mesh,
        in_specs=(P("row", None), P("col", None)),
        out_specs=(P("row"), P("col"), P("row", "col")),
        check_vma=False,
    )
```

time: 498 us -> 64.4 us (0.13)
  blocking collectives: 424 us -> 0 us
  Pallas kernels: 0 us -> 59.7 us
  waiting for transfers between devices: 25.2 us -> 0 us
  other arithmetic: 22.4 us -> 0 us
  between operations: 14.2 us -> 0.64 us
  matrix products: 8.12 us -> 0 us
    pmax x4 -> x0, blocking collectives: 206 us -> none  [the longest x2 124 us: caption_lse(): top = lax.pmax(local_max, 'row')]
    psum x4 -> x0, blocking collectives: 161 us -> none  [the longest x2 114 us: caption_lse(): total = lax.psum(jnp.sum(jnp.exp(logits - top[None, :]), axis=0), 'row')]
    pallas_call x0 -> x1, Pallas kernels: none -> 59.7 us  [per_device(): pl.pallas_call(functools.partial(kernel, rows_n, cols_n), out_shape=(jax....]
    all_gather x2 -> x0, blocking collectives: 57.7 us -> none  [joined(): gathered = jax.tree.map(lambda a: lax.all_gather(a, axis), part)]
    all_gather x1 -> x0, waiting for transfers between devices: 25.2 us -> none  [joined(): gathered = jax.tree.map(lambda a: lax.all_gather(a, axis), part)]
    add x30 -> x0, other arithmetic: 19.4 us -> none  [the longest x15 19 us: combine_three(): first[2] * left[:, None] + second[2] * right[:, None]]
    dot_general x2 -> x0, matrix products: 8.12 us -> none  [the longest x1 4.1 us: per_device(): jnp.dot(weights.astype(jnp.bfloat16), captions, preferred_element_type=jn...]
  transfers between devices with their start and end apart: 1 -> 0, of which waited for: 1 -> 0; matrix products, arithmetic and copies ran while one was open for 0% -> 0% of each run, Pallas kernels for 0% -> 0%
where the time goes in v1:
time: 64.4 us; the launch traced here: 64.1 us
  Pallas kernels  59.7 us (93%)
  local copies, waits for them, and re-layouts  3.8 us (6%)
    pallas_call x1, Pallas kernels, per_device(): pl.pallas_call(functools.partial(kernel, rows_n, cols_n), out_shape=(jax....  59.7 us
    unnamed x3, local copies, waits for them, and re-layouts  3.8 us

profile of v1, /device:TPU:1, one launch (start us, length us, event | category | flops | bytes accessed | tf_op | source)
XLA Modules:
  0.0 64.1 jit_solution(13846339830475447388)
XLA Ops:
  0.6 59.7 %sinkhorn.1 = (f32[1,128]{1,0:T(1,128)}, f32[16,128]{1,0:T(8,128)}, f32[72,128]{1,0:T(8,128)}) custom-call(bf16[128,1152]{1,0:T(8,128)(2,1)} %images_hbm.1, bf16[2048,1152]{1,0:T(8,128)(2,1)} %captions_hbm.1), custom_call_target="tpu_custom_call" | custom-call | tf_op jit(solution)/shard_map/sinkhorn/pallas_call | solution.py:231
  60.3 1.1 %copy.8 = f32[128]{0:T(128)} copy(f32[128]{0:T(128)} %bitcast.5) | data formatting | bytes 1024
  61.4 1.3 %copy.9 = f32[2048]{0:T(1024)} copy(f32[2048]{0:T(1024)} %bitcast.4) | data formatting | bytes 16384
  62.7 1.4 %copy.10 = f32[128,72]{0,1:T(8,128)} copy(f32[128,72]{0,1:T(8,128)} %bitcast.3) | data formatting | bytes 73728

commit v2 on v1

v2 whole, which is shorter than its diff:
```python
import functools
import math

import jax
import jax.numpy as jnp
from jax import lax
from jax.experimental import pallas as pl
from jax.experimental.pallas import tpu as pltpu
from jax.sharding import PartitionSpec as P

MESH = pl.DeviceIdType.MESH
ENTROPIC = 0.05
LOG2E = math.log2(math.e)
ITERS = 2
LANES = 128
GROUP = 16
CHUNK = 512
X_CHIPS = 4


def ring(offset, size):
    return min(offset, size - offset)


def tree(op, values):
    values = list(values)
    while len(values) > 1:
        rest = [op(a, b) for a, b in zip(values[::2], values[1::2])]
        values = rest + ([values[-1]] if len(values) % 2 else [])
    return values[0]


def lse_of(parts):
    top = tree(jnp.maximum, parts)
    return top + jnp.log2(tree(jnp.add, [jnp.exp2(p - top) for p in parts]))


def send(src, dst, ssem, rsem, device):
    pltpu.make_async_remote_copy(
        src_ref=src, dst_ref=dst, send_sem=ssem, recv_sem=rsem,
        device_id=device, device_id_type=MESH,
    ).start()


def drain(ref, sem):
    pltpu.make_async_copy(ref, ref, sem).wait()


def greet(barrier, device):
    pl.semaphore_signal(barrier, inc=1, device_id=device, device_id_type=MESH)


def kernel(
    rows_n, cols_n, images_hbm, captions_hbm, image_out, caption_out, mapped_out,
    images, captions, score, weights, stat_max, stat_sum, block_max, block_sum, dual,
    image_src, image_recv, caption_src, caption_recv, tail_src, tail_recv, numer, pair_recv, y_src, y_recv,
    load_sem, image_ssem, image_rsem, caption_ssem, caption_rsem, tail_ssem, tail_rsem,
    pair_ssem, pair_rsem, y_ssem, y_rsem,
):
    here, width = images.shape
    blocks = score.shape[1] // LANES
    loads = captions.shape[0] // CHUNK
    x_n = X_CHIPS
    z_n = rows_n // x_n
    y_n = cols_n // 2
    share = width // cols_n
    r, c = lax.axis_index("row"), lax.axis_index("col")
    z, x, y, core = r // x_n, lax.rem(r, x_n), c // 2, lax.rem(c, 2)

    def row_peer(dz, dx):
        return (lax.rem(z + dz, z_n) * x_n + lax.rem(x + dx, x_n), c)

    def col_peer(dy, dc):
        return (r, lax.rem(y + dy, y_n) * 2 + lax.rem(core + dc, 2))

    row_peers = sorted(
        [(dz, dx) for dz in range(z_n) for dx in range(x_n) if dz or dx],
        key=lambda p: -ring(p[0], z_n) - ring(p[1], x_n),
    )
    col_peers = sorted(
        [(dy, dc) for dy in range(y_n) for dc in range(2) if dy or dc],
        key=lambda p: (p[0] > 0, -ring(p[0], y_n), p[1]),
    )
    first = y_n // 4
    made = [(first + q) % y_n for q in range(y_n)]
    y_order = sorted(range(y_n), key=lambda p: (-ring(p, y_n), made.index(p)))

    image_load = pltpu.make_async_copy(images_hbm, images, load_sem.at[loads])
    image_load.start()
    caption_loads = []
    for b in range(loads):
        part = pl.ds(b * CHUNK, CHUNK)
        caption_loads.append(
            pltpu.make_async_copy(captions_hbm.at[part], captions.at[part], load_sem.at[b])
        )
        caption_loads[-1].start()

    barrier = pltpu.get_barrier_semaphore()
    for p in row_peers:
        greet(barrier, row_peer(*p))
    for p in col_peers:
        greet(barrier, col_peer(*p))

    image_load.wait()
    for b in range(loads):
        caption_loads[b].wait()
        part = pl.ds(b * CHUNK, CHUNK)
        score[:, part] = lax.dot_general(
            images[...], captions[part, :], (((1,), (1,)), ((), ())),
            preferred_element_type=jnp.float32,
        ) * jnp.float32(LOG2E / ENTROPIC)
        for g in range(here // GROUP):
            rows = pl.ds(g * GROUP, GROUP)
            logits = [
                score[rows, pl.ds(b * CHUNK + i * LANES, LANES)] for i in range(CHUNK // LANES)
            ]
            top = tree(jnp.maximum, logits)
            if b:
                old = stat_max[rows, :]
                top = jnp.maximum(top, old)
            total = tree(jnp.add, [jnp.exp2(v - top) for v in logits])
            if b:
                total = total + stat_sum[rows, :] * jnp.exp2(old - top)
            stat_max[rows, :] = top
            stat_sum[rows, :] = total

    log_a = jnp.float32(-math.log2(here * rows_n))
    log_b = jnp.float32(-math.log2(score.shape[1] * cols_n))

    def logit_rows(g):
        rows = pl.ds(g * GROUP, GROUP)
        return rows, [
            score[rows, pl.ds(b * LANES, LANES)] + dual[pl.ds(b, 1), :] for b in range(blocks)
        ]

    def send_image(step):
        for k, p in enumerate(col_peers):
            send(
                image_src.at[step], image_recv.at[step, k],
                image_ssem.at[step], image_rsem.at[step], col_peer(*p),
            )

    def get_image(step):
        drain(image_recv.at[step], image_rsem.at[step])
        return lse_of(
            [image_src[step]] + [image_recv[step, k] for k in range(len(col_peers))]
        )

    for step in range(ITERS):
        for g in range(here // GROUP if step else 0):
            rows, logits = logit_rows(g)
            top = tree(jnp.maximum, logits)
            stat_max[rows, :] = top
            stat_sum[rows, :] = tree(jnp.add, [jnp.exp2(v - top) for v in logits])
        lane_max = stat_max[...].T
        top = jnp.max(lane_max, axis=0, keepdims=True)
        total = jnp.sum(stat_sum[...].T * jnp.exp2(lane_max - top), axis=0, keepdims=True)
        image_src[step] = top + jnp.log2(total)
        if step == 0:
            pl.semaphore_wait(barrier, len(row_peers) + len(col_peers))
        send_image(step)
        image_dual = log_a - get_image(step)
        if step == ITERS - 1:
            image_out[...] = image_dual * jnp.float32(ENTROPIC / LOG2E)
        column = jnp.broadcast_to(image_dual, (LANES, here)).T
        for b in range(blocks):
            logits = score[:, pl.ds(b * LANES, LANES)] + column
            top = jnp.max(logits, axis=0, keepdims=True)
            block_max[pl.ds(b, 1), :] = top
            block_sum[pl.ds(b, 1), :] = jnp.sum(jnp.exp2(logits - top), axis=0, keepdims=True)
        caption_src[step] = block_max[...] + jnp.log2(block_sum[...])
        for k, p in enumerate(row_peers):
            send(
                caption_src.at[step], caption_recv.at[step, k],
                caption_ssem.at[step], caption_rsem.at[step], row_peer(*p),
            )
        drain(caption_recv.at[step], caption_rsem.at[step])
        dual[...] = log_b - lse_of(
            [caption_src[step]] + [caption_recv[step, k] for k in range(len(row_peers))]
        )

    caption_out[...] = dual[...] * jnp.float32(ENTROPIC / LOG2E)
    for g in range(here // GROUP):
        rows, logits = logit_rows(g)
        top = jnp.max(tree(jnp.maximum, logits), axis=1, keepdims=True)
        stat_max[rows, :] = jnp.broadcast_to(top, (GROUP, LANES))
        terms = [jnp.exp2(v - top) for v in logits]
        stat_sum[rows, :] = tree(jnp.add, terms)
        for b, w in enumerate(terms):
            weights[rows, pl.ds(b * LANES, LANES)] = w.astype(jnp.bfloat16)
    tail_src[0:1, :] = stat_max[...].T[0:1, :]
    tail_src[1:2, :] = jnp.sum(stat_sum[...].T, axis=0, keepdims=True)
    for k, p in enumerate(col_peers):
        send(tail_src, tail_recv.at[k], tail_ssem, tail_rsem.at[min(k, 1)], col_peer(*p))

    def chunk(dy, of_core):
        start = (lax.rem(y + dy, y_n) * 2 + of_core) * share
        return pl.ds(pl.multiple_of(start, 8), share)

    width_blocks = width // LANES
    reach = [0]
    for q in range(y_n):
        ends = [(2 * share * at) % LANES + 2 * share * (q + 1) for at in range(y_n)]
        reach.append(min(width_blocks, -(-max(ends) // LANES)))
    start = 2 * share * lax.rem(y + first, y_n) // LANES
    for q, dy in enumerate(made):
        for i in range(reach[q], reach[q + 1]):
            block = lax.rem(start + i, width_blocks) * LANES
            part = pl.ds(pl.multiple_of(block, LANES), LANES)
            numer[part, :] = jnp.dot(
                weights[...], captions[:, part], preferred_element_type=jnp.float32
            ).T
        part = chunk(dy, 1 - core)
        send(numer.at[part], pair_recv.at[dy], pair_ssem, pair_rsem.at[dy], col_peer(0, 1))

    drain(tail_recv.at[0], tail_rsem.at[0])
    own_top, other_top = tail_src[0:1, :], tail_recv[0, 0:1, :]
    pair_top = jnp.maximum(own_top, other_top)
    own_scale, other_scale = jnp.exp2(own_top - pair_top), jnp.exp2(other_top - pair_top)
    for dy in y_order:
        drain(pair_recv.at[dy], pair_rsem.at[dy])
        y_src[dy] = numer[chunk(dy, core), :] * own_scale + pair_recv[dy] * other_scale
        if dy:
            send(y_src.at[dy], y_recv.at[dy - 1], y_ssem, y_rsem.at[dy - 1], col_peer(dy, 0))

    rest = tail_recv.at[pl.ds(1, len(col_peers) - 1)]
    drain(rest, tail_rsem.at[1])
    senders = [((y_n - dy) % y_n, dc) for dy, dc in col_peers]
    tops = {p: tail_recv[k, 0:1, :] for k, p in enumerate(senders)}
    masses = {p: tail_recv[k, 1:2, :] for k, p in enumerate(senders)}
    tops[0, 0], masses[0, 0] = own_top, tail_src[1:2, :]
    top = tree(jnp.maximum, list(tops.values()))
    mass = tree(jnp.add, [masses[p] * jnp.exp2(tops[p] - top) for p in tops])
    inverse = 1.0 / mass
    factor = [
        jnp.exp2(jnp.maximum(tops[dy, 0], tops[dy, 1]) - top) * inverse for dy in range(y_n)
    ]
    total = y_src[0] * factor[0]
    for dy in sorted(range(1, y_n), key=lambda p: ring(p, y_n)):
        sender = y_n - dy
        drain(y_recv.at[dy - 1], y_rsem.at[dy - 1])
        total = total + y_recv[dy - 1] * factor[sender]
    mapped_out[...] = total

    for step in range(ITERS):
        drain(image_recv.at[step], image_ssem.at[step])
    drain(tail_recv, tail_ssem)
    for step in range(ITERS):
        drain(caption_recv.at[step], caption_ssem.at[step])
    drain(pair_recv, pair_ssem)
    drain(y_recv, y_ssem)


def place(image_dual, caption_dual, mapped, image_out, caption_out, mapped_out, sems):
    pairs = ((mapped, mapped_out), (caption_dual, caption_out), (image_dual, image_out))
    copies = [pltpu.make_async_copy(a, b, sems.at[i]) for i, (a, b) in enumerate(pairs)]
    for copy in copies:
        copy.start()
    for copy in copies:
        copy.wait()


def solution(mesh):
    rows_n, cols_n = mesh.shape["row"], mesh.shape["col"]
    y_n = cols_n // 2

    def per_device(images, captions):
        here, width = images.shape
        cols = captions.shape[0]
        share = width // cols_n
        blocks = cols // LANES
        f32 = jnp.float32
        vmem = pl.BlockSpec(memory_space=pltpu.VMEM)
        dma = pltpu.SemaphoreType.DMA
        shapes = ((1, here), (blocks, LANES), (share, here))
        parts = pl.pallas_call(
            functools.partial(kernel, rows_n, cols_n),
            out_shape=tuple(pltpu.VMEM(shape, f32) for shape in shapes),
            in_specs=[pl.BlockSpec(memory_space=pl.ANY)] * 2,
            out_specs=(vmem, vmem, vmem),
            scratch_shapes=[
                pltpu.VMEM((here, width), jnp.bfloat16),
                pltpu.VMEM((cols, width), jnp.bfloat16),
                pltpu.VMEM((here, cols), f32),
                pltpu.VMEM((here, cols), jnp.bfloat16),
                pltpu.VMEM((here, LANES), f32),
                pltpu.VMEM((here, LANES), f32),
                pltpu.VMEM((blocks, LANES), f32),
                pltpu.VMEM((blocks, LANES), f32),
                pltpu.VMEM((blocks, LANES), f32),
                pltpu.VMEM((ITERS, 1, here), f32),
                pltpu.VMEM((ITERS, cols_n - 1, 1, here), f32),
                pltpu.VMEM((ITERS, blocks, LANES), f32),
                pltpu.VMEM((ITERS, rows_n - 1, blocks, LANES), f32),
                pltpu.VMEM((2, here), f32),
                pltpu.VMEM((cols_n - 1, 2, here), f32),
                pltpu.VMEM((width, here), f32),
                pltpu.VMEM((y_n, share, here), f32),
                pltpu.VMEM((y_n, share, here), f32),
                pltpu.VMEM((y_n - 1, share, here), f32),
                dma((cols // CHUNK + 1,)),
                dma((ITERS,)),
                dma((ITERS,)),
                dma((ITERS,)),
                dma((ITERS,)),
                dma,
                dma((2,)),
                dma,
                dma((y_n,)),
                dma,
                dma((y_n - 1,)),
            ],
            compiler_params=pltpu.CompilerParams(
                collective_id=0, has_side_effects=True, vmem_limit_bytes=60 * 2**20
            ),
            name="sinkhorn",
        )(images, captions)
        image_dual, caption_dual, mapped = pl.pallas_call(
            place,
            out_shape=tuple(jax.ShapeDtypeStruct(shape, f32) for shape in shapes),
            in_specs=[vmem] * 3,
            out_specs=[pl.BlockSpec(memory_space=pl.ANY)] * 3,
            scratch_shapes=[dma((3,))],
            name="place",
        )(*[pltpu.with_memory_space_constraint(p, pltpu.VMEM) for p in parts])
        return image_dual.reshape(here), caption_dual.reshape(cols), mapped.T

    return jax.shard_map(
        per_device,
        mesh=mesh,
        in_specs=(P("row", None), P("col", None)),
        out_specs=(P("row"), P("col"), P("row", "col")),
        check_vma=False,
    )
```

time: 64.4 us -> 55.3 us (0.86)
  Pallas kernels: 59.7 us -> 54.3 us
  local copies, waits for them, and re-layouts: 3.8 us -> 0 us
    pallas_call x1 -> x2, Pallas kernels: 59.7 us -> 54.3 us  [the longest x1 53.7 us: per_device(): pl.pallas_call(functools.partial(kernel, rows_n, cols_n), out_shape=tuple...]
    unnamed x3 -> x0, local copies, waits for them, and re-layouts: 3.8 us -> none
where the time goes in v2:
time: 55.3 us; the launch traced here: 55 us
  Pallas kernels  54.3 us (98%)
  between operations  0.64 us (1%)
    pallas_call x1, Pallas kernels, per_device(): pl.pallas_call(functools.partial(kernel, rows_n, cols_n), out_shape=tuple...  53.7 us

profile of v2, /device:TPU:1, one launch (start us, length us, event | category | flops | bytes accessed | tf_op | source)
XLA Modules:
  0.0 55.0 jit_solution(11384488867826693869)
XLA Ops:
  0.6 53.7 %sinkhorn.1 = (f32[1,128]{1,0:T(1,128)S(1)}, f32[16,128]{1,0:T(8,128)S(1)}, f32[72,128]{1,0:T(8,128)S(1)}) custom-call(bf16[128,1152]{1,0:T(8,128)(2,1)} %images_hbm.1, bf16[2048,1152]{1,0:T(8,128)(2,1)} %captions_hbm.1), custom_call_target="tpu_custom_call" | custom-call | tf_op jit(solution)/shard_map/sinkhorn/pallas_call | solution.py:276
  54.3 0.6 %place.1 = (f32[1,128]{1,0:T(1,128)}, f32[16,128]{1,0:T(8,128)}, f32[72,128]{1,0:T(8,128)}) custom-call(f32[1,128]{1,0:T(1,128)S(1)} %get-tuple-element.9.image_dual, f32[16,128]{1,0:T(8,128)S(1)} %get-tuple-element.10.caption_dual, f32[72,128]{1,0:T(8,128)S(1)} %get-tuple-element.11.mapped), custom_call_target="tpu_custom_call" | custom-call | tf_op jit(solution)/shard_map/place/pallas_call | solution.py:318

commit v3 on v2

--- a/solution.py
+++ b/solution.py
@@ -81,9 +81,7 @@
         [(dy, dc) for dy in range(y_n) for dc in range(2) if dy or dc],
         key=lambda p: (p[0] > 0, -ring(p[0], y_n), p[1]),
     )
-    first = y_n // 4
-    made = [(first + q) % y_n for q in range(y_n)]
-    y_order = sorted(range(y_n), key=lambda p: (-ring(p, y_n), made.index(p)))
+    y_order = list(range(y_n // 2)) + list(range(y_n // 2, y_n))[::-1]
 
     image_load = pltpu.make_async_copy(images_hbm, images, load_sem.at[loads])
     image_load.start()
@@ -144,6 +142,12 @@
         drain(image_recv.at[step], image_rsem.at[step])
         return lse_of(
             [image_src[step]] + [image_recv[step, k] for k in range(len(col_peers))]
+        )
+
+    def send_caption(step, slot, device):
+        send(
+            caption_src.at[step], caption_recv.at[step, slot],
+            caption_ssem.at[step], caption_rsem.at[step], device,
         )
 
     for step in range(ITERS):
@@ -169,11 +173,19 @@
             block_max[pl.ds(b, 1), :] = top
             block_sum[pl.ds(b, 1), :] = jnp.sum(jnp.exp2(logits - top), axis=0, keepdims=True)
         caption_src[step] = block_max[...] + jnp.log2(block_sum[...])
-        for k, p in enumerate(row_peers):
-            send(
-                caption_src.at[step], caption_recv.at[step, k],
-                caption_ssem.at[step], caption_rsem.at[step], row_peer(*p),
-            )
+        if step < ITERS - 1:
+            for k, p in enumerate(row_peers):
+                send_caption(step, k, row_peer(*p))
+        else:
+            for zt in range(z_n):
+                dz = lax.rem(zt - z + z_n, z_n)
+                for dx in sorted(range(1, x_n), key=lambda p: -ring(p, x_n)):
+                    send_caption(step, dz * x_n + dx - 1, row_peer(dz, dx))
+
+                @pl.when(dz != 0)
+                def _():
+                    send_caption(step, dz * x_n - 1, row_peer(dz, 0))
+
         drain(caption_recv.at[step], caption_rsem.at[step])
         dual[...] = log_b - lse_of(
             [caption_src[step]] + [caption_recv[step, k] for k in range(len(row_peers))]
@@ -188,67 +200,61 @@
         stat_sum[rows, :] = tree(jnp.add, terms)
         for b, w in enumerate(terms):
             weights[rows, pl.ds(b * LANES, LANES)] = w.astype(jnp.bfloat16)
-    tail_src[0:1, :] = stat_max[...].T[0:1, :]
-    tail_src[1:2, :] = jnp.sum(stat_sum[...].T, axis=0, keepdims=True)
-    for k, p in enumerate(col_peers):
-        send(tail_src, tail_recv.at[k], tail_ssem, tail_rsem.at[min(k, 1)], col_peer(*p))
-
-    def chunk(dy, of_core):
-        start = (lax.rem(y + dy, y_n) * 2 + of_core) * share
-        return pl.ds(pl.multiple_of(start, 8), share)
-
-    width_blocks = width // LANES
-    reach = [0]
-    for q in range(y_n):
-        ends = [(2 * share * at) % LANES + 2 * share * (q + 1) for at in range(y_n)]
-        reach.append(min(width_blocks, -(-max(ends) // LANES)))
-    start = 2 * share * lax.rem(y + first, y_n) // LANES
-    for q, dy in enumerate(made):
-        for i in range(reach[q], reach[q + 1]):
-            block = lax.rem(start + i, width_blocks) * LANES
-            part = pl.ds(pl.multiple_of(block, LANES), LANES)
-            numer[part, :] = jnp.dot(
-                weights[...], captions[:, part], preferred_element_type=jnp.float32
-            ).T
-        part = chunk(dy, 1 - core)
-        send(numer.at[part], pair_recv.at[dy], pair_ssem, pair_rsem.at[dy], col_peer(0, 1))
-
-    drain(tail_recv.at[0], tail_rsem.at[0])
-    own_top, other_top = tail_src[0:1, :], tail_recv[0, 0:1, :]
-    pair_top = jnp.maximum(own_top, other_top)
-    own_scale, other_scale = jnp.exp2(own_top - pair_top), jnp.exp2(other_top - pair_top)
-    for dy in y_order:
-        drain(pair_recv.at[dy], pair_rsem.at[dy])
-        y_src[dy] = numer[chunk(dy, core), :] * own_scale + pair_recv[dy] * other_scale
-        if dy:
-            send(y_src.at[dy], y_recv.at[dy - 1], y_ssem, y_rsem.at[dy - 1], col_peer(dy, 0))
-
-    rest = tail_recv.at[pl.ds(1, len(col_peers) - 1)]
-    drain(rest, tail_rsem.at[1])
-    senders = [((y_n - dy) % y_n, dc) for dy, dc in col_peers]
-    tops = {p: tail_recv[k, 0:1, :] for k, p in enumerate(senders)}
-    masses = {p: tail_recv[k, 1:2, :] for k, p in enumerate(senders)}
-    tops[0, 0], masses[0, 0] = own_top, tail_src[1:2, :]
-    top = tree(jnp.maximum, list(tops.values()))
-    mass = tree(jnp.add, [masses[p] * jnp.exp2(tops[p] - top) for p in tops])
+    def chunk(yt, of_core):
+        return pl.ds(pl.multiple_of((2 * yt + of_core) * share, 8), share)
+
+    made = set()
+    for q, yt in enumerate(y_order):
+        for b in range(2 * share * yt // LANES, -(-2 * share * (yt + 1) // LANES)):
+            if b not in made:
+                made.add(b)
+                part = pl.ds(b * LANES, LANES)
+                numer[part, :] = jnp.dot(
+                    weights[...], captions[:, part], preferred_element_type=jnp.float32
+                ).T
+        send(
+            numer.at[chunk(yt, 1 - core)], pair_recv.at[yt],
+            pair_ssem, pair_rsem.at[yt], col_peer(0, 1),
+        )
+        if q == 0:
+            own = tail_recv.at[c]
+            own[0:1, :] = stat_max[...].T[0:1, :]
+            own[1:2, :] = jnp.sum(stat_sum[...].T, axis=0, keepdims=True)
+            tail_src[...] = own[...]
+            for k, p in enumerate(col_peers):
+                send(tail_src, tail_recv.at[c], tail_ssem, tail_rsem.at[min(k, 1)], col_peer(*p))
+
+    other = tail_recv.at[c + 1 - 2 * core]
+    drain(other, tail_rsem.at[0])
+    pair_top = jnp.maximum(tail_src[0:1, :], other[0:1, :])
+    own_scale = jnp.exp2(tail_src[0:1, :] - pair_top)
+    other_scale = jnp.exp2(other[0:1, :] - pair_top)
+    for yt in y_order:
+        drain(pair_recv.at[yt], pair_rsem.at[yt])
+        y_src[yt] = numer[chunk(yt, core), :] * own_scale + pair_recv[yt] * other_scale
+
+        @pl.when(yt != y)
+        def _():
+            send(y_src.at[yt], y_recv.at[y], y_ssem, y_rsem, (r, 2 * yt + core))
+
+    y_recv[y] = y_src[y]
+    drain(tail_recv.at[pl.ds(0, cols_n - 2)], tail_rsem.at[1])
+    tops = [tail_recv[k, 0:1, :] for k in range(cols_n)]
+    top = tree(jnp.maximum, tops)
+    mass = tree(jnp.add, [tail_recv[k, 1:2, :] * jnp.exp2(tops[k] - top) for k in range(cols_n)])
     inverse = 1.0 / mass
     factor = [
-        jnp.exp2(jnp.maximum(tops[dy, 0], tops[dy, 1]) - top) * inverse for dy in range(y_n)
+        jnp.exp2(jnp.maximum(tops[2 * k], tops[2 * k + 1]) - top) * inverse for k in range(y_n)
     ]
-    total = y_src[0] * factor[0]
-    for dy in sorted(range(1, y_n), key=lambda p: ring(p, y_n)):
-        sender = y_n - dy
-        drain(y_recv.at[dy - 1], y_rsem.at[dy - 1])
-        total = total + y_recv[dy - 1] * factor[sender]
-    mapped_out[...] = total
-
+    drain(y_recv.at[pl.ds(0, y_n - 1)], y_rsem)
+    mapped_out[...] = tree(jnp.add, [y_recv[k] * factor[k] for k in range(y_n)])
+
+    drain(tail_recv.at[pl.ds(0, cols_n - 1)], tail_ssem)
+    drain(pair_recv, pair_ssem)
+    drain(y_recv.at[pl.ds(0, y_n - 1)], y_ssem)
     for step in range(ITERS):
         drain(image_recv.at[step], image_ssem.at[step])
-    drain(tail_recv, tail_ssem)
-    for step in range(ITERS):
         drain(caption_recv.at[step], caption_ssem.at[step])
-    drain(pair_recv, pair_ssem)
-    drain(y_recv, y_ssem)
 
 
 def place(image_dual, caption_dual, mapped, image_out, caption_out, mapped_out, sems):
@@ -293,11 +299,11 @@
                 pltpu.VMEM((ITERS, blocks, LANES), f32),
                 pltpu.VMEM((ITERS, rows_n - 1, blocks, LANES), f32),
                 pltpu.VMEM((2, here), f32),
-                pltpu.VMEM((cols_n - 1, 2, here), f32),
+                pltpu.VMEM((cols_n, 2, here), f32),
                 pltpu.VMEM((width, here), f32),
                 pltpu.VMEM((y_n, share, here), f32),
                 pltpu.VMEM((y_n, share, here), f32),
-                pltpu.VMEM((y_n - 1, share, here), f32),
+                pltpu.VMEM((y_n, share, here), f32),
                 dma((cols // CHUNK + 1,)),
                 dma((ITERS,)),
                 dma((ITERS,)),
@@ -308,7 +314,7 @@
                 dma,
                 dma((y_n,)),
                 dma,
-                dma((y_n - 1,)),
+                dma,
             ],
             compiler_params=pltpu.CompilerParams(
                 collective_id=0, has_side_effects=True, vmem_limit_bytes=60 * 2**20

time: 55.3 us -> 53.8 us (0.973)
  Pallas kernels: 54.3 us -> 52.4 us
    pallas_call x1, Pallas kernels: 53.7 us -> 51.8 us  [per_device(): pl.pallas_call(functools.partial(kernel, rows_n, cols_n), out_shape=tuple...]
where the time goes in v3:
time: 53.8 us; the launch traced here: 53.1 us
  Pallas kernels  52.4 us (97%)
  between operations  0.64 us (1%)
    pallas_call x1, Pallas kernels, per_device(): pl.pallas_call(functools.partial(kernel, rows_n, cols_n), out_shape=tuple...  51.8 us

profile of v3, /device:TPU:1, one launch (start us, length us, event | category | flops | bytes accessed | tf_op | source)
XLA Modules:
  0.0 53.1 jit_solution(1234300356000192249)
XLA Ops:
  0.6 51.8 %sinkhorn.1 = (f32[1,128]{1,0:T(1,128)S(1)}, f32[16,128]{1,0:T(8,128)S(1)}, f32[72,128]{1,0:T(8,128)S(1)}) custom-call(bf16[128,1152]{1,0:T(8,128)(2,1)} %images_hbm.1, bf16[2048,1152]{1,0:T(8,128)(2,1)} %captions_hbm.1), custom_call_target="tpu_custom_call" | custom-call | tf_op jit(solution)/shard_map/sinkhorn/pallas_call | solution.py:282
  52.4 0.6 %place.1 = (f32[1,128]{1,0:T(1,128)}, f32[16,128]{1,0:T(8,128)}, f32[72,128]{1,0:T(8,128)}) custom-call(f32[1,128]{1,0:T(1,128)S(1)} %get-tuple-element.9.image_dual, f32[16,128]{1,0:T(8,128)S(1)} %get-tuple-element.10.caption_dual, f32[72,128]{1,0:T(8,128)S(1)} %get-tuple-element.11.mapped), custom_call_target="tpu_custom_call" | custom-call | tf_op jit(solution)/shard_map/place/pallas_call | solution.py:324

commit v4 on v3

--- a/solution.py
+++ b/solution.py
@@ -16,6 +16,8 @@
 GROUP = 16
 CHUNK = 512
 X_CHIPS = 4
+KIND = ('xz', 'xz')
+ZORDER = ('far', 'abs')
 
 
 def ring(offset, size):
@@ -53,8 +55,8 @@
 def kernel(
     rows_n, cols_n, images_hbm, captions_hbm, image_out, caption_out, mapped_out,
     images, captions, score, weights, stat_max, stat_sum, block_max, block_sum, dual,
-    image_src, image_recv, caption_src, caption_recv, tail_src, tail_recv, numer, pair_recv, y_src, y_recv,
-    load_sem, image_ssem, image_rsem, caption_ssem, caption_rsem, tail_ssem, tail_rsem,
+    image_src, image_recv, caption_src, caption_recv, plane_src, plane_recv, tail_src, tail_recv, numer, pair_recv, y_src, y_recv,
+    load_sem, image_ssem, image_rsem, caption_ssem, caption_rsem, plane_ssem, plane_rsem, tail_ssem, tail_rsem,
     pair_ssem, pair_rsem, y_ssem, y_rsem,
 ):
     here, width = images.shape
@@ -73,6 +75,8 @@
     def col_peer(dy, dc):
         return (r, lax.rem(y + dy, y_n) * 2 + lax.rem(core + dc, 2))
 
+    x_peers = sorted(range(1, x_n), key=lambda p: -ring(p, x_n))
+    z_peers = sorted(range(1, z_n), key=lambda p: -ring(p, z_n))
     row_peers = sorted(
         [(dz, dx) for dz in range(z_n) for dx in range(x_n) if dz or dx],
         key=lambda p: -ring(p[0], z_n) - ring(p[1], x_n),
@@ -81,7 +85,7 @@
         [(dy, dc) for dy in range(y_n) for dc in range(2) if dy or dc],
         key=lambda p: (p[0] > 0, -ring(p[0], y_n), p[1]),
     )
-    y_order = list(range(y_n // 2)) + list(range(y_n // 2, y_n))[::-1]
+    y_order = [0, 1, 2, 3, 4, 5, 6, 7]
 
     image_load = pltpu.make_async_copy(images_hbm, images, load_sem.at[loads])
     image_load.start()
@@ -149,6 +153,57 @@
             caption_src.at[step], caption_recv.at[step, slot],
             caption_ssem.at[step], caption_rsem.at[step], device,
         )
+
+    def send_plane(step, slot, device):
+        send(
+            plane_src.at[step], plane_recv.at[step, slot],
+            plane_ssem.at[step], plane_rsem.at[step], device,
+        )
+
+    def to_z(step, put, slot_of):
+        if ZORDER[step] == "far":
+            for dz in z_peers:
+                put(step, slot_of(dz), row_peer(dz, 0))
+        else:
+            for zt in range(z_n):
+                dz = lax.rem(zt - z + z_n, z_n)
+
+                @pl.when(dz != 0)
+                def _():
+                    put(step, slot_of(dz), row_peer(dz, 0))
+
+    def to_x(step, put):
+        for dx in x_peers:
+            put(step, dx - 1, row_peer(0, dx))
+
+    def exchange_caption(step):
+        own = caption_src[step]
+        if KIND[step] == "direct":
+            for zt in range(z_n):
+                dz = lax.rem(zt - z + z_n, z_n)
+                for dx in x_peers:
+                    send_caption(step, dz * x_n + dx - 1, row_peer(dz, dx))
+
+                @pl.when(dz != 0)
+                def _():
+                    send_caption(step, dz * x_n - 1, row_peer(dz, 0))
+
+            drain(caption_recv.at[step], caption_rsem.at[step])
+            return lse_of([own] + [caption_recv[step, k] for k in range(len(row_peers))])
+        n, m = (x_n - 1, z_n - 1) if KIND[step] == "xz" else (z_n - 1, x_n - 1)
+        if KIND[step] == "xz":
+            to_x(step, send_caption)
+        else:
+            to_z(step, send_caption, lambda dz: dz - 1)
+        drain(caption_recv.at[step, pl.ds(0, n)], caption_rsem.at[step])
+        plane = lse_of([own] + [caption_recv[step, k] for k in range(n)])
+        plane_src[step] = plane
+        if KIND[step] == "xz":
+            to_z(step, send_plane, lambda dz: dz - 1)
+        else:
+            to_x(step, send_plane)
+        drain(plane_recv.at[step, pl.ds(0, m)], plane_rsem.at[step])
+        return lse_of([plane] + [plane_recv[step, k] for k in range(m)])
 
     for step in range(ITERS):
         for g in range(here // GROUP if step else 0):
@@ -173,23 +228,7 @@
             block_max[pl.ds(b, 1), :] = top
             block_sum[pl.ds(b, 1), :] = jnp.sum(jnp.exp2(logits - top), axis=0, keepdims=True)
         caption_src[step] = block_max[...] + jnp.log2(block_sum[...])
-        if step < ITERS - 1:
-            for k, p in enumerate(row_peers):
-                send_caption(step, k, row_peer(*p))
-        else:
-            for zt in range(z_n):
-                dz = lax.rem(zt - z + z_n, z_n)
-                for dx in sorted(range(1, x_n), key=lambda p: -ring(p, x_n)):
-                    send_caption(step, dz * x_n + dx - 1, row_peer(dz, dx))
-
-                @pl.when(dz != 0)
-                def _():
-                    send_caption(step, dz * x_n - 1, row_peer(dz, 0))
-
-        drain(caption_recv.at[step], caption_rsem.at[step])
-        dual[...] = log_b - lse_of(
-            [caption_src[step]] + [caption_recv[step, k] for k in range(len(row_peers))]
-        )
+        dual[...] = log_b - exchange_caption(step)
 
     caption_out[...] = dual[...] * jnp.float32(ENTROPIC / LOG2E)
     for g in range(here // GROUP):
@@ -254,7 +293,12 @@
     drain(y_recv.at[pl.ds(0, y_n - 1)], y_ssem)
     for step in range(ITERS):
         drain(image_recv.at[step], image_ssem.at[step])
-        drain(caption_recv.at[step], caption_ssem.at[step])
+        if KIND[step] == "direct":
+            drain(caption_recv.at[step], caption_ssem.at[step])
+        else:
+            n, m = (x_n - 1, z_n - 1) if KIND[step] == "xz" else (z_n - 1, x_n - 1)
+            drain(caption_recv.at[step, pl.ds(0, n)], caption_ssem.at[step])
+            drain(plane_recv.at[step, pl.ds(0, m)], plane_ssem.at[step])
 
 
 def place(image_dual, caption_dual, mapped, image_out, caption_out, mapped_out, sems):
@@ -298,6 +342,8 @@
                 pltpu.VMEM((ITERS, cols_n - 1, 1, here), f32),
                 pltpu.VMEM((ITERS, blocks, LANES), f32),
                 pltpu.VMEM((ITERS, rows_n - 1, blocks, LANES), f32),
+                pltpu.VMEM((ITERS, blocks, LANES), f32),
+                pltpu.VMEM((ITERS, rows_n // X_CHIPS + X_CHIPS, blocks, LANES), f32),
                 pltpu.VMEM((2, here), f32),
                 pltpu.VMEM((cols_n, 2, here), f32),
                 pltpu.VMEM((width, here), f32),
@@ -305,6 +351,8 @@
                 pltpu.VMEM((y_n, share, here), f32),
                 pltpu.VMEM((y_n, share, here), f32),
                 dma((cols // CHUNK + 1,)),
+                dma((ITERS,)),
+                dma((ITERS,)),
                 dma((ITERS,)),
                 dma((ITERS,)),
                 dma((ITERS,)),

time: 53.8 us -> 53.5 us (level)
  no operation moved by 1% of the time
where the time goes in v4:
time: 53.5 us; the launch traced here: 52.8 us
  Pallas kernels  52.1 us (97%)
  between operations  0.64 us (1%)
    pallas_call x1, Pallas kernels, per_device(): pl.pallas_call(functools.partial(kernel, rows_n, cols_n), out_shape=tuple...  51.5 us

profile of v4, /device:TPU:1, one launch (start us, length us, event | category | flops | bytes accessed | tf_op | source)
XLA Modules:
  0.0 52.8 jit_solution(3501241431020269522)
XLA Ops:
  0.6 51.5 %sinkhorn.1 = (f32[1,128]{1,0:T(1,128)S(1)}, f32[16,128]{1,0:T(8,128)S(1)}, f32[72,128]{1,0:T(8,128)S(1)}) custom-call(bf16[128,1152]{1,0:T(8,128)(2,1)} %images_hbm.1, bf16[2048,1152]{1,0:T(8,128)(2,1)} %captions_hbm.1), custom_call_target="tpu_custom_call" | custom-call | tf_op jit(solution)/shard_map/sinkhorn/pallas_call | solution.py:326
  52.1 0.6 %place.1 = (f32[1,128]{1,0:T(1,128)}, f32[16,128]{1,0:T(8,128)}, f32[72,128]{1,0:T(8,128)}) custom-call(f32[1,128]{1,0:T(1,128)S(1)} %get-tuple-element.9.image_dual, f32[16,128]{1,0:T(8,128)S(1)} %get-tuple-element.10.caption_dual, f32[72,128]{1,0:T(8,128)S(1)} %get-tuple-element.11.mapped), custom_call_target="tpu_custom_call" | custom-call | tf_op jit(solution)/shard_map/place/pallas_call | solution.py:372

commit v5 on v3

--- a/solution.py
+++ b/solution.py
@@ -16,6 +16,7 @@
 GROUP = 16
 CHUNK = 512
 X_CHIPS = 4
+EARLY = (0,)
 
 
 def ring(offset, size):
@@ -53,8 +54,9 @@
 def kernel(
     rows_n, cols_n, images_hbm, captions_hbm, image_out, caption_out, mapped_out,
     images, captions, score, weights, stat_max, stat_sum, block_max, block_sum, dual,
-    image_src, image_recv, caption_src, caption_recv, tail_src, tail_recv, numer, pair_recv, y_src, y_recv,
-    load_sem, image_ssem, image_rsem, caption_ssem, caption_rsem, tail_ssem, tail_rsem,
+    image_src, image_recv, caption_src, x_recv, plane_src, z_recv, early_recv, joined, tail_src, tail_recv, numer, pair_recv, y_src, y_recv,
+    load_sem, image_ssem, image_rsem, x_ssem, x_rsem, z_ssem, z_rsem,
+    early_ssem, early_rsem, tail_ssem, tail_rsem,
     pair_ssem, pair_rsem, y_ssem, y_rsem,
 ):
     here, width = images.shape
@@ -73,15 +75,13 @@
     def col_peer(dy, dc):
         return (r, lax.rem(y + dy, y_n) * 2 + lax.rem(core + dc, 2))
 
-    row_peers = sorted(
-        [(dz, dx) for dz in range(z_n) for dx in range(x_n) if dz or dx],
-        key=lambda p: -ring(p[0], z_n) - ring(p[1], x_n),
-    )
+    x_peers = sorted(range(1, x_n), key=lambda p: -ring(p, x_n))
+    early = functools.reduce(jnp.logical_or, [z == zt for zt in EARLY])
     col_peers = sorted(
         [(dy, dc) for dy in range(y_n) for dc in range(2) if dy or dc],
         key=lambda p: (p[0] > 0, -ring(p[0], y_n), p[1]),
     )
-    y_order = list(range(y_n // 2)) + list(range(y_n // 2, y_n))[::-1]
+    y_order = list(range(y_n))
 
     image_load = pltpu.make_async_copy(images_hbm, images, load_sem.at[loads])
     image_load.start()
@@ -94,8 +94,17 @@
         caption_loads[-1].start()
 
     barrier = pltpu.get_barrier_semaphore()
-    for p in row_peers:
-        greet(barrier, row_peer(*p))
+    for dz in range(1, z_n):
+        greet(barrier, row_peer(dz, 0))
+    for dx in x_peers:
+        greet(barrier, row_peer(0, dx))
+
+    @pl.when(early)
+    def _():
+        for dz in range(1, z_n):
+            for dx in x_peers:
+                greet(barrier, row_peer(dz, dx))
+
     for p in col_peers:
         greet(barrier, col_peer(*p))
 
@@ -144,11 +153,55 @@
             [image_src[step]] + [image_recv[step, k] for k in range(len(col_peers))]
         )
 
-    def send_caption(step, slot, device):
-        send(
-            caption_src.at[step], caption_recv.at[step, slot],
-            caption_ssem.at[step], caption_rsem.at[step], device,
-        )
+    def exchange_caption(step):
+        last = step == ITERS - 1
+        if last:
+            for zt in EARLY:
+                dz = lax.rem(zt - z + z_n, z_n)
+
+                @pl.when(dz != 0)
+                def _():
+                    for dx in x_peers + [0]:
+                        send(
+                            caption_src.at[step], early_recv.at[(dz - 1) * x_n + dx],
+                            early_ssem, early_rsem, row_peer(dz, dx),
+                        )
+
+        for dx in x_peers:
+            send(
+                caption_src.at[step], x_recv.at[step, dx - 1],
+                x_ssem.at[step], x_rsem.at[step], row_peer(0, dx),
+            )
+        drain(x_recv.at[step], x_rsem.at[step])
+        plane = lse_of([caption_src[step]] + [x_recv[step, k] for k in range(x_n - 1)])
+        plane_src[step] = plane
+        for zt in range(z_n):
+            if last and zt in EARLY:
+                continue
+            dz = lax.rem(zt - z + z_n, z_n)
+
+            @pl.when(dz != 0)
+            def _():
+                send(
+                    plane_src.at[step], z_recv.at[step, dz - 1],
+                    z_ssem.at[step], z_rsem.at[step], row_peer(dz, 0),
+                )
+
+        if not last:
+            drain(z_recv.at[step], z_rsem.at[step])
+            return lse_of([plane] + [z_recv[step, k] for k in range(z_n - 1)])
+
+        @pl.when(jnp.logical_not(early))
+        def _():
+            drain(z_recv.at[step], z_rsem.at[step])
+            joined[...] = lse_of([plane] + [z_recv[step, k] for k in range(z_n - 1)])
+
+        @pl.when(early)
+        def _():
+            drain(early_recv, early_rsem)
+            joined[...] = lse_of([plane] + [early_recv[k] for k in range(early_recv.shape[0])])
+
+        return joined[...]
 
     for step in range(ITERS):
         for g in range(here // GROUP if step else 0):
@@ -161,7 +214,9 @@
         total = jnp.sum(stat_sum[...].T * jnp.exp2(lane_max - top), axis=0, keepdims=True)
         image_src[step] = top + jnp.log2(total)
         if step == 0:
-            pl.semaphore_wait(barrier, len(row_peers) + len(col_peers))
+            near = z_n + x_n - 2 + len(col_peers)
+            others = (x_n - 1) * (len(EARLY) - early.astype(jnp.int32))
+            pl.semaphore_wait(barrier, near + others)
         send_image(step)
         image_dual = log_a - get_image(step)
         if step == ITERS - 1:
@@ -173,23 +228,7 @@
             block_max[pl.ds(b, 1), :] = top
             block_sum[pl.ds(b, 1), :] = jnp.sum(jnp.exp2(logits - top), axis=0, keepdims=True)
         caption_src[step] = block_max[...] + jnp.log2(block_sum[...])
-        if step < ITERS - 1:
-            for k, p in enumerate(row_peers):
-                send_caption(step, k, row_peer(*p))
-        else:
-            for zt in range(z_n):
-                dz = lax.rem(zt - z + z_n, z_n)
-                for dx in sorted(range(1, x_n), key=lambda p: -ring(p, x_n)):
-                    send_caption(step, dz * x_n + dx - 1, row_peer(dz, dx))
-
-                @pl.when(dz != 0)
-                def _():
-                    send_caption(step, dz * x_n - 1, row_peer(dz, 0))
-
-        drain(caption_recv.at[step], caption_rsem.at[step])
-        dual[...] = log_b - lse_of(
-            [caption_src[step]] + [caption_recv[step, k] for k in range(len(row_peers))]
-        )
+        dual[...] = log_b - exchange_caption(step)
 
     caption_out[...] = dual[...] * jnp.float32(ENTROPIC / LOG2E)
     for g in range(here // GROUP):
@@ -254,7 +293,20 @@
     drain(y_recv.at[pl.ds(0, y_n - 1)], y_ssem)
     for step in range(ITERS):
         drain(image_recv.at[step], image_ssem.at[step])
-        drain(caption_recv.at[step], caption_ssem.at[step])
+        drain(x_recv.at[step], x_ssem.at[step])
+    for step in range(ITERS - 1):
+        drain(z_recv.at[step], z_ssem.at[step])
+
+    @pl.when(early)
+    def _():
+        drain(z_recv.at[ITERS - 1, pl.ds(0, z_n - len(EARLY))], z_ssem.at[ITERS - 1])
+        if len(EARLY) > 1:
+            drain(early_recv.at[pl.ds(0, (len(EARLY) - 1) * x_n)], early_ssem)
+
+    @pl.when(jnp.logical_not(early))
+    def _():
+        drain(z_recv.at[ITERS - 1, pl.ds(0, z_n - 1 - len(EARLY))], z_ssem.at[ITERS - 1])
+        drain(early_recv.at[pl.ds(0, len(EARLY) * x_n)], early_ssem)
 
 
 def place(image_dual, caption_dual, mapped, image_out, caption_out, mapped_out, sems):
@@ -297,7 +349,11 @@
                 pltpu.VMEM((ITERS, 1, here), f32),
                 pltpu.VMEM((ITERS, cols_n - 1, 1, here), f32),
                 pltpu.VMEM((ITERS, blocks, LANES), f32),
-                pltpu.VMEM((ITERS, rows_n - 1, blocks, LANES), f32),
+                pltpu.VMEM((ITERS, X_CHIPS - 1, blocks, LANES), f32),
+                pltpu.VMEM((ITERS, blocks, LANES), f32),
+                pltpu.VMEM((ITERS, rows_n // X_CHIPS - 1, blocks, LANES), f32),
+                pltpu.VMEM((rows_n - X_CHIPS, blocks, LANES), f32),
+                pltpu.VMEM((blocks, LANES), f32),
                 pltpu.VMEM((2, here), f32),
                 pltpu.VMEM((cols_n, 2, here), f32),
                 pltpu.VMEM((width, here), f32),
@@ -309,6 +365,10 @@
                 dma((ITERS,)),
                 dma((ITERS,)),
                 dma((ITERS,)),
+                dma((ITERS,)),
+                dma((ITERS,)),
+                dma,
+                dma,
                 dma,
                 dma((2,)),
                 dma,

time: 53.8 us -> 51.1 us (0.950)
  Pallas kernels: 52.4 us -> 50 us
    pallas_call x1, Pallas kernels: 51.8 us -> 49.4 us  [per_device(): pl.pallas_call(functools.partial(kernel, rows_n, cols_n), out_shape=tuple...]
where the time goes in v5:
time: 51.1 us; the launch traced here: 50.7 us
  Pallas kernels  50 us (98%)
  between operations  0.64 us (1%)
    pallas_call x1, Pallas kernels, per_device(): pl.pallas_call(functools.partial(kernel, rows_n, cols_n), out_shape=tuple...  49.4 us

profile of v5, /device:TPU:1, one launch (start us, length us, event | category | flops | bytes accessed | tf_op | source)
XLA Modules:
  0.0 50.7 jit_solution(8057009752474173144)
XLA Ops:
  0.6 49.4 %sinkhorn.1 = (f32[1,128]{1,0:T(1,128)S(1)}, f32[16,128]{1,0:T(8,128)S(1)}, f32[72,128]{1,0:T(8,128)S(1)}) custom-call(bf16[128,1152]{1,0:T(8,128)(2,1)} %images_hbm.1, bf16[2048,1152]{1,0:T(8,128)(2,1)} %captions_hbm.1), custom_call_target="tpu_custom_call" | custom-call | tf_op jit(solution)/shard_map/sinkhorn/pallas_call | solution.py:334
  50.0 0.6 %place.1 = (f32[1,128]{1,0:T(1,128)}, f32[16,128]{1,0:T(8,128)}, f32[72,128]{1,0:T(8,128)}) custom-call(f32[1,128]{1,0:T(1,128)S(1)} %get-tuple-element.9.image_dual, f32[16,128]{1,0:T(8,128)S(1)} %get-tuple-element.10.caption_dual, f32[72,128]{1,0:T(8,128)S(1)} %get-tuple-element.11.mapped), custom_call_target="tpu_custom_call" | custom-call | tf_op jit(solution)/shard_map/place/pallas_call | solution.py:384

commit v6 on v3

--- a/solution.py
+++ b/solution.py
@@ -53,8 +53,10 @@
 def kernel(
     rows_n, cols_n, images_hbm, captions_hbm, image_out, caption_out, mapped_out,
     images, captions, score, weights, stat_max, stat_sum, block_max, block_sum, dual,
-    image_src, image_recv, caption_src, caption_recv, tail_src, tail_recv, numer, pair_recv, y_src, y_recv,
-    load_sem, image_ssem, image_rsem, caption_ssem, caption_rsem, tail_ssem, tail_rsem,
+    image_src, image_recv, caption_src, x_recv, cross_recv, plane_src, cross_src, z_recv, first_recv,
+    tail_src, tail_recv, numer, pair_recv, y_src, y_recv,
+    load_sem, image_ssem, image_rsem, x_ssem, x_rsem, cross_rsem, z_ssem, z_rsem,
+    first_ssem, first_rsem, tail_ssem, tail_rsem,
     pair_ssem, pair_rsem, y_ssem, y_rsem,
 ):
     here, width = images.shape
@@ -70,18 +72,18 @@
     def row_peer(dz, dx):
         return (lax.rem(z + dz, z_n) * x_n + lax.rem(x + dx, x_n), c)
 
+    def cross_peer(dz, dx):
+        return (row_peer(dz, dx)[0], c + 1 - 2 * core)
+
     def col_peer(dy, dc):
         return (r, lax.rem(y + dy, y_n) * 2 + lax.rem(core + dc, 2))
 
-    row_peers = sorted(
-        [(dz, dx) for dz in range(z_n) for dx in range(x_n) if dz or dx],
-        key=lambda p: -ring(p[0], z_n) - ring(p[1], x_n),
-    )
+    x_peers = sorted(range(1, x_n), key=lambda p: -ring(p, x_n))
     col_peers = sorted(
         [(dy, dc) for dy in range(y_n) for dc in range(2) if dy or dc],
         key=lambda p: (p[0] > 0, -ring(p[0], y_n), p[1]),
     )
-    y_order = list(range(y_n // 2)) + list(range(y_n // 2, y_n))[::-1]
+    y_order = list(range(y_n))
 
     image_load = pltpu.make_async_copy(images_hbm, images, load_sem.at[loads])
     image_load.start()
@@ -94,8 +96,32 @@
         caption_loads[-1].start()
 
     barrier = pltpu.get_barrier_semaphore()
-    for p in row_peers:
-        greet(barrier, row_peer(*p))
+    z_peers = sorted(range(1, z_n), key=lambda p: -ring(p, z_n))
+
+    @pl.when(core == 0)
+    def _():
+        for dz in z_peers:
+            greet(barrier, cross_peer(dz, 0))
+
+    @pl.when(core != 0)
+    def _():
+        for dz in z_peers:
+            greet(barrier, row_peer(dz, 0))
+        for dx in x_peers:
+            greet(barrier, row_peer(0, dx))
+            greet(barrier, cross_peer(0, dx))
+
+    @pl.when(z == 0)
+    def _():
+        for dz in z_peers:
+            for dx in x_peers:
+                greet(barrier, row_peer(dz, dx))
+
+    @pl.when(jnp.logical_and(z == 0, core == 0))
+    def _():
+        for dz in z_peers:
+            greet(barrier, row_peer(dz, 0))
+
     for p in col_peers:
         greet(barrier, col_peer(*p))
 
@@ -144,11 +170,86 @@
             [image_src[step]] + [image_recv[step, k] for k in range(len(col_peers))]
         )
 
-    def send_caption(step, slot, device):
+    def send_first(step):
+        dz = lax.rem(z_n - z, z_n)
+        for dx in x_peers + [0]:
+            send(
+                caption_src.at[step], first_recv.at[(dz - 1) * x_n + dx],
+                first_ssem, first_rsem, row_peer(dz, dx),
+            )
+
+    def send_planes(step, src, of_peer):
+        for zt in range(1 if step == ITERS - 1 else 0, z_n):
+            dz = lax.rem(zt - z + z_n, z_n)
+
+            @pl.when(dz != 0)
+            def _():
+                send(
+                    src.at[step], z_recv.at[step, dz - 1],
+                    z_ssem.at[step], z_rsem.at[step], of_peer(dz, 0),
+                )
+
+    def join(step, count, parts):
+        drain(z_recv.at[step, pl.ds(0, count)], z_rsem.at[step])
+        dual[...] = log_b - lse_of(parts + [z_recv[step, k] for k in range(count)])
+
+    def join_first(parts):
+        drain(first_recv, first_rsem)
+        dual[...] = log_b - lse_of(parts + [first_recv[k] for k in range(first_recv.shape[0])])
+
+    def exchange_zero(step):
+        last = step == ITERS - 1
+        if last:
+            pl.when(z != 0)(functools.partial(send_first, step))
+        for dx in x_peers + [0]:
+            send(
+                caption_src.at[step], cross_recv.at[step, dx],
+                x_ssem.at[step], cross_rsem.at[step], cross_peer(0, dx),
+            )
+
+        def normal():
+            join(step, z_n, [])
+
+        if not last:
+            normal()
+            return
+        pl.when(z != 0)(normal)
+
+        @pl.when(z == 0)
+        def _():
+            sibling = z_recv.at[step, z_n - 1]
+            drain(sibling, z_rsem.at[step])
+            join_first([sibling[...]])
+
+    def exchange_one(step):
+        last = step == ITERS - 1
+        if last:
+            pl.when(z != 0)(functools.partial(send_first, step))
+        for dx in x_peers:
+            send(
+                caption_src.at[step], x_recv.at[step, dx - 1],
+                x_ssem.at[step], x_rsem.at[step], row_peer(0, dx),
+            )
+        drain(x_recv.at[step], x_rsem.at[step])
+        plane = lse_of([caption_src[step]] + [x_recv[step, k] for k in range(x_n - 1)])
+        plane_src[step] = plane
+        send_planes(step, plane_src, row_peer)
+        drain(cross_recv.at[step], cross_rsem.at[step])
+        cross_src[step] = lse_of([cross_recv[step, k] for k in range(x_n)])
+        send_planes(step, cross_src, cross_peer)
         send(
-            caption_src.at[step], caption_recv.at[step, slot],
-            caption_ssem.at[step], caption_rsem.at[step], device,
+            cross_src.at[step], z_recv.at[step, z_n - 1],
+            z_ssem.at[step], z_rsem.at[step], cross_peer(0, 0),
         )
+
+        def normal():
+            join(step, z_n - 1, [plane])
+
+        if last:
+            pl.when(z != 0)(normal)
+            pl.when(z == 0)(functools.partial(join_first, [plane]))
+        else:
+            normal()
 
     for step in range(ITERS):
         for g in range(here // GROUP if step else 0):
@@ -161,35 +262,26 @@
         total = jnp.sum(stat_sum[...].T * jnp.exp2(lane_max - top), axis=0, keepdims=True)
         image_src[step] = top + jnp.log2(total)
         if step == 0:
-            pl.semaphore_wait(barrier, len(row_peers) + len(col_peers))
+            from_zero = x_n - 1 + jnp.where(z == 0, 0, x_n)
+            from_one = x_n - 1 + 2 * (z_n - 1) + jnp.where(z == 0, 0, x_n - 1)
+            pl.semaphore_wait(barrier, len(col_peers) + jnp.where(core == 0, from_zero, from_one))
         send_image(step)
         image_dual = log_a - get_image(step)
         if step == ITERS - 1:
             image_out[...] = image_dual * jnp.float32(ENTROPIC / LOG2E)
         column = jnp.broadcast_to(image_dual, (LANES, here)).T
         for b in range(blocks):
+            block_max[pl.ds(b, 1), :] = jnp.max(
+                score[:, pl.ds(b * LANES, LANES)] + column, axis=0, keepdims=True
+            )
+        for b in range(blocks):
             logits = score[:, pl.ds(b * LANES, LANES)] + column
-            top = jnp.max(logits, axis=0, keepdims=True)
-            block_max[pl.ds(b, 1), :] = top
-            block_sum[pl.ds(b, 1), :] = jnp.sum(jnp.exp2(logits - top), axis=0, keepdims=True)
+            block_sum[pl.ds(b, 1), :] = jnp.sum(
+                jnp.exp2(logits - block_max[pl.ds(b, 1), :]), axis=0, keepdims=True
+            )
         caption_src[step] = block_max[...] + jnp.log2(block_sum[...])
-        if step < ITERS - 1:
-            for k, p in enumerate(row_peers):
-                send_caption(step, k, row_peer(*p))
-        else:
-            for zt in range(z_n):
-                dz = lax.rem(zt - z + z_n, z_n)
-                for dx in sorted(range(1, x_n), key=lambda p: -ring(p, x_n)):
-                    send_caption(step, dz * x_n + dx - 1, row_peer(dz, dx))
-
-                @pl.when(dz != 0)
-                def _():
-                    send_caption(step, dz * x_n - 1, row_peer(dz, 0))
-
-        drain(caption_recv.at[step], caption_rsem.at[step])
-        dual[...] = log_b - lse_of(
-            [caption_src[step]] + [caption_recv[step, k] for k in range(len(row_peers))]
-        )
+        pl.when(core == 0)(functools.partial(exchange_zero, step))
+        pl.when(core != 0)(functools.partial(exchange_one, step))
 
     caption_out[...] = dual[...] * jnp.float32(ENTROPIC / LOG2E)
     for g in range(here // GROUP):
@@ -200,6 +292,9 @@
         stat_sum[rows, :] = tree(jnp.add, terms)
         for b, w in enumerate(terms):
             weights[rows, pl.ds(b * LANES, LANES)] = w.astype(jnp.bfloat16)
+    tail_src[0:1, :] = stat_max[...].T[0:1, :]
+    tail_src[1:2, :] = jnp.sum(stat_sum[...].T, axis=0, keepdims=True)
+
     def chunk(yt, of_core):
         return pl.ds(pl.multiple_of((2 * yt + of_core) * share, 8), share)
 
@@ -213,14 +308,11 @@
                     weights[...], captions[:, part], preferred_element_type=jnp.float32
                 ).T
         send(
-            numer.at[chunk(yt, 1 - core)], pair_recv.at[yt],
+            numer.at[chunk(yt, core)], pair_recv.at[yt],
             pair_ssem, pair_rsem.at[yt], col_peer(0, 1),
         )
         if q == 0:
-            own = tail_recv.at[c]
-            own[0:1, :] = stat_max[...].T[0:1, :]
-            own[1:2, :] = jnp.sum(stat_sum[...].T, axis=0, keepdims=True)
-            tail_src[...] = own[...]
+            tail_recv[c] = tail_src[...]
             for k, p in enumerate(col_peers):
                 send(tail_src, tail_recv.at[c], tail_ssem, tail_rsem.at[min(k, 1)], col_peer(*p))
 
@@ -231,13 +323,9 @@
     other_scale = jnp.exp2(other[0:1, :] - pair_top)
     for yt in y_order:
         drain(pair_recv.at[yt], pair_rsem.at[yt])
-        y_src[yt] = numer[chunk(yt, core), :] * own_scale + pair_recv[yt] * other_scale
-
-        @pl.when(yt != y)
-        def _():
-            send(y_src.at[yt], y_recv.at[y], y_ssem, y_rsem, (r, 2 * yt + core))
-
-    y_recv[y] = y_src[y]
+        y_src[yt] = numer[chunk(yt, 1 - core), :] * own_scale + pair_recv[yt] * other_scale
+        send(y_src.at[yt], y_recv.at[y], y_ssem, y_rsem, (r, 2 * yt + 1 - core))
+
     drain(tail_recv.at[pl.ds(0, cols_n - 2)], tail_rsem.at[1])
     tops = [tail_recv[k, 0:1, :] for k in range(cols_n)]
     top = tree(jnp.maximum, tops)
@@ -246,15 +334,38 @@
     factor = [
         jnp.exp2(jnp.maximum(tops[2 * k], tops[2 * k + 1]) - top) * inverse for k in range(y_n)
     ]
-    drain(y_recv.at[pl.ds(0, y_n - 1)], y_rsem)
+    drain(y_recv, y_rsem)
     mapped_out[...] = tree(jnp.add, [y_recv[k] * factor[k] for k in range(y_n)])
 
     drain(tail_recv.at[pl.ds(0, cols_n - 1)], tail_ssem)
     drain(pair_recv, pair_ssem)
-    drain(y_recv.at[pl.ds(0, y_n - 1)], y_ssem)
+    drain(y_recv, y_ssem)
     for step in range(ITERS):
         drain(image_recv.at[step], image_ssem.at[step])
-        drain(caption_recv.at[step], caption_ssem.at[step])
+
+    @pl.when(z != 0)
+    def _():
+        drain(first_recv.at[pl.ds(0, x_n)], first_ssem)
+
+    @pl.when(core == 0)
+    def _():
+        for step in range(ITERS):
+            drain(cross_recv.at[step], x_ssem.at[step])
+
+    @pl.when(core != 0)
+    def _():
+        for step in range(ITERS):
+            drain(x_recv.at[step], x_ssem.at[step])
+        for step in range(ITERS - 1):
+            drain(first_recv.at[pl.ds(0, 2 * z_n - 1)], z_ssem.at[step])
+
+        @pl.when(z == 0)
+        def _():
+            drain(first_recv.at[pl.ds(0, 2 * z_n - 1)], z_ssem.at[ITERS - 1])
+
+        @pl.when(z != 0)
+        def _():
+            drain(first_recv.at[pl.ds(0, 2 * z_n - 3)], z_ssem.at[ITERS - 1])
 
 
 def place(image_dual, caption_dual, mapped, image_out, caption_out, mapped_out, sems):
@@ -297,7 +408,12 @@
                 pltpu.VMEM((ITERS, 1, here), f32),
                 pltpu.VMEM((ITERS, cols_n - 1, 1, here), f32),
                 pltpu.VMEM((ITERS, blocks, LANES), f32),
-                pltpu.VMEM((ITERS, rows_n - 1, blocks, LANES), f32),
+                pltpu.VMEM((ITERS, X_CHIPS - 1, blocks, LANES), f32),
+                pltpu.VMEM((ITERS, X_CHIPS, blocks, LANES), f32),
+                pltpu.VMEM((ITERS, blocks, LANES), f32),
+                pltpu.VMEM((ITERS, blocks, LANES), f32),
+                pltpu.VMEM((ITERS, rows_n // X_CHIPS, blocks, LANES), f32),
+                pltpu.VMEM((rows_n - X_CHIPS, blocks, LANES), f32),
                 pltpu.VMEM((2, here), f32),
                 pltpu.VMEM((cols_n, 2, here), f32),
                 pltpu.VMEM((width, here), f32),
@@ -309,6 +425,11 @@
                 dma((ITERS,)),
                 dma((ITERS,)),
                 dma((ITERS,)),
+                dma((ITERS,)),
+                dma((ITERS,)),
+                dma((ITERS,)),
+                dma,
+                dma,
                 dma,
                 dma((2,)),
                 dma,

time: 53.8 us -> 50.3 us (0.935); the launches traced: 53.1 us -> 50.2 us
  Pallas kernels: 52.4 us -> 49.5 us
    pallas_call x1, Pallas kernels: 51.8 us -> 48.9 us  [per_device(): pl.pallas_call(functools.partial(kernel, rows_n, cols_n), out_shape=tuple...]
where the time goes in v6:
time: 50.3 us; the launch traced here: 50.2 us
  Pallas kernels  49.5 us (98%)
  between operations  0.64 us (1%)
    pallas_call x1, Pallas kernels, per_device(): pl.pallas_call(functools.partial(kernel, rows_n, cols_n), out_shape=tuple...  48.9 us

profile of v6, /device:TPU:1, one launch (start us, length us, event | category | flops | bytes accessed | tf_op | source)
XLA Modules:
  0.0 50.2 jit_solution(14622488167349712231)
XLA Ops:
  0.6 48.9 %sinkhorn.1 = (f32[1,128]{1,0:T(1,128)S(1)}, f32[16,128]{1,0:T(8,128)S(1)}, f32[72,128]{1,0:T(8,128)S(1)}) custom-call(bf16[128,1152]{1,0:T(8,128)(2,1)} %images_hbm.1, bf16[2048,1152]{1,0:T(8,128)(2,1)} %captions_hbm.1), custom_call_target="tpu_custom_call" | custom-call | tf_op jit(solution)/shard_map/sinkhorn/pallas_call | solution.py:393
  49.5 0.6 %place.1 = (f32[1,128]{1,0:T(1,128)}, f32[16,128]{1,0:T(8,128)}, f32[72,128]{1,0:T(8,128)}) custom-call(f32[1,128]{1,0:T(1,128)S(1)} %get-tuple-element.9.image_dual, f32[16,128]{1,0:T(8,128)S(1)} %get-tuple-element.10.caption_dual, f32[72,128]{1,0:T(8,128)S(1)} %get-tuple-element.11.mapped), custom_call_target="tpu_custom_call" | custom-call | tf_op jit(solution)/shard_map/place/pallas_call | solution.py:445

commit v7 on v6

--- a/solution.py
+++ b/solution.py
@@ -172,7 +172,8 @@
 
     def send_first(step):
         dz = lax.rem(z_n - z, z_n)
-        for dx in x_peers + [0]:
+        for xt in range(x_n):
+            dx = lax.rem(xt - x + x_n, x_n)
             send(
                 caption_src.at[step], first_recv.at[(dz - 1) * x_n + dx],
                 first_ssem, first_rsem, row_peer(dz, dx),
@@ -313,8 +314,9 @@
         )
         if q == 0:
             tail_recv[c] = tail_src[...]
-            for k, p in enumerate(col_peers):
-                send(tail_src, tail_recv.at[c], tail_ssem, tail_rsem.at[min(k, 1)], col_peer(*p))
+            send(tail_src, tail_recv.at[c], tail_ssem, tail_rsem.at[0], col_peer(0, 1))
+    for p in col_peers[1:]:
+        send(tail_src, tail_recv.at[c], tail_ssem, tail_rsem.at[1], col_peer(*p))
 
     other = tail_recv.at[c + 1 - 2 * core]
     drain(other, tail_rsem.at[0])

time: 50.3 us -> 50.3 us (level)
  no operation moved by 1% of the time
where the time goes in v7:
time: 50.3 us; the launch traced here: 50.2 us
  Pallas kernels  49.5 us (98%)
  between operations  0.64 us (1%)
    pallas_call x1, Pallas kernels, per_device(): pl.pallas_call(functools.partial(kernel, rows_n, cols_n), out_shape=tuple...  48.9 us

profile of v7, /device:TPU:1, one launch (start us, length us, event | category | flops | bytes accessed | tf_op | source)
XLA Modules:
  0.0 50.2 jit_solution(5279443849394082780)
XLA Ops:
  0.6 48.9 %sinkhorn.1 = (f32[1,128]{1,0:T(1,128)S(1)}, f32[16,128]{1,0:T(8,128)S(1)}, f32[72,128]{1,0:T(8,128)S(1)}) custom-call(bf16[128,1152]{1,0:T(8,128)(2,1)} %images_hbm.1, bf16[2048,1152]{1,0:T(8,128)(2,1)} %captions_hbm.1), custom_call_target="tpu_custom_call" | custom-call | tf_op jit(solution)/shard_map/sinkhorn/pallas_call | solution.py:395
  49.5 0.6 %place.1 = (f32[1,128]{1,0:T(1,128)}, f32[16,128]{1,0:T(8,128)}, f32[72,128]{1,0:T(8,128)}) custom-call(f32[1,128]{1,0:T(1,128)S(1)} %get-tuple-element.9.image_dual, f32[16,128]{1,0:T(8,128)S(1)} %get-tuple-element.10.caption_dual, f32[72,128]{1,0:T(8,128)S(1)} %get-tuple-element.11.mapped), custom_call_target="tpu_custom_call" | custom-call | tf_op jit(solution)/shard_map/place/pallas_call | solution.py:447

commit v8 on v7

--- a/solution.py
+++ b/solution.py
@@ -14,6 +14,7 @@
 ITERS = 2
 LANES = 128
 GROUP = 16
+STEP = 8
 CHUNK = 512
 X_CHIPS = 4
 
@@ -133,8 +134,8 @@
             images[...], captions[part, :], (((1,), (1,)), ((), ())),
             preferred_element_type=jnp.float32,
         ) * jnp.float32(LOG2E / ENTROPIC)
-        for g in range(here // GROUP):
-            rows = pl.ds(g * GROUP, GROUP)
+        for g in range(here // STEP):
+            rows = pl.ds(g * STEP, STEP)
             logits = [
                 score[rows, pl.ds(b * CHUNK + i * LANES, LANES)] for i in range(CHUNK // LANES)
             ]
@@ -151,8 +152,8 @@
     log_a = jnp.float32(-math.log2(here * rows_n))
     log_b = jnp.float32(-math.log2(score.shape[1] * cols_n))
 
-    def logit_rows(g):
-        rows = pl.ds(g * GROUP, GROUP)
+    def logit_rows(g, size):
+        rows = pl.ds(g * size, size)
         return rows, [
             score[rows, pl.ds(b * LANES, LANES)] + dual[pl.ds(b, 1), :] for b in range(blocks)
         ]
@@ -253,8 +254,8 @@
             normal()
 
     for step in range(ITERS):
-        for g in range(here // GROUP if step else 0):
-            rows, logits = logit_rows(g)
+        for g in range(here // STEP if step else 0):
+            rows, logits = logit_rows(g, STEP)
             top = tree(jnp.maximum, logits)
             stat_max[rows, :] = top
             stat_sum[rows, :] = tree(jnp.add, [jnp.exp2(v - top) for v in logits])
@@ -286,7 +287,7 @@
 
     caption_out[...] = dual[...] * jnp.float32(ENTROPIC / LOG2E)
     for g in range(here // GROUP):
-        rows, logits = logit_rows(g)
+        rows, logits = logit_rows(g, GROUP)
         top = jnp.max(tree(jnp.maximum, logits), axis=1, keepdims=True)
         stat_max[rows, :] = jnp.broadcast_to(top, (GROUP, LANES))
         terms = [jnp.exp2(v - top) for v in logits]

time: 50.3 us -> 50.3 us (level)
  no operation moved by 1% of the time
where the time goes in v8:
time: 50.3 us; the launch traced here: 50.2 us
  Pallas kernels  49.5 us (98%)
  between operations  0.64 us (1%)
    pallas_call x1, Pallas kernels, per_device(): pl.pallas_call(functools.partial(kernel, rows_n, cols_n), out_shape=tuple...  48.9 us

profile of v8, /device:TPU:1, one launch (start us, length us, event | category | flops | bytes accessed | tf_op | source)
XLA Modules:
  0.0 50.2 jit_solution(10497644085555317818)
XLA Ops:
  0.6 48.9 %sinkhorn.1 = (f32[1,128]{1,0:T(1,128)S(1)}, f32[16,128]{1,0:T(8,128)S(1)}, f32[72,128]{1,0:T(8,128)S(1)}) custom-call(bf16[128,1152]{1,0:T(8,128)(2,1)} %images_hbm.1, bf16[2048,1152]{1,0:T(8,128)(2,1)} %captions_hbm.1), custom_call_target="tpu_custom_call" | custom-call | tf_op jit(solution)/shard_map/sinkhorn/pallas_call | solution.py:396
  49.5 0.6 %place.1 = (f32[1,128]{1,0:T(1,128)}, f32[16,128]{1,0:T(8,128)}, f32[72,128]{1,0:T(8,128)}) custom-call(f32[1,128]{1,0:T(1,128)S(1)} %get-tuple-element.9.image_dual, f32[16,128]{1,0:T(8,128)S(1)} %get-tuple-element.10.caption_dual, f32[72,128]{1,0:T(8,128)S(1)} %get-tuple-element.11.mapped), custom_call_target="tpu_custom_call" | custom-call | tf_op jit(solution)/shard_map/place/pallas_call | solution.py:448
